TPU v7x, 128 devices: a whole 4x4x4 slice. The times are simulated.
128 devices in a mesh: dp: 8 (over z, y_hi), ctx: 16 (over x, y_lo, core).
Axes of the slice: x: 4, y: 4 (y_hi: 2, y_lo: 2; y = y_hi * 2 + y_lo), z: 4, core: 2. Of those that a mesh axis runs over, the one named last changes fastest.
Arguments:
- inputs: bfloat16 [8, 4096, 1536], P('dp', 'ctx'), may hold values from -6 to 6
- block_ids: int32 [8, 32], P('dp'), may hold values from 0 to 2, never falling along the last dimension, each value on 1 to 24 neighbouring positions
- attn_gain: float32 [1536], replicated, may hold values from 0.1 to 1.9
- w_qkv: bfloat16 [1536, 2304], replicated, may hold values from -6 to 6
- w_out: bfloat16 [768, 1536], replicated, may hold values from -0.21875 to 0.21875
- conv_gain: float32 [1536], replicated, may hold values from 0.1 to 1.9
- conv_in: bfloat16 [1536, 3072], P(None, 'dp'), may hold values from -0.15625 to 0.15625
- depthwise_w: float32 [31, 1536], replicated, may hold values from -1 to 1
- depth_gain: float32 [1536], replicated, may hold values from 0.1 to 1.9
- conv_out: bfloat16 [1536, 1536], replicated, may hold values from -0.15625 to 0.15625
Outputs:
- output: bfloat16 [8, 4096, 1536], P('dp', 'ctx')
Inputs may be any that keep to these rules, and one draw needn't show every extreme that they name: `block_ids`: utterance numbers never fall along a row; a row holds 3 utterances of 1 to 24 blocks, one of exactly 24 blocks.
All inputs are finite; a program needn't handle non-finite values.
Results may differ from a plain program's by a relative error of at most 0.01.
Values may be sent and summed in bfloat16 or wider, within the bound.
A program may use at most 192 MiB of HBM per device.

v0:
```python
import functools
import math

import jax
import jax.numpy as jnp
import numpy as np
from jax import lax
from jax.experimental import pallas as pl
from jax.experimental.pallas import tpu as pltpu
from jax.sharding import PartitionSpec as P

MODEL_DIM = 1536
HEAD_COUNT = 8
HEAD_DIM = 96
HALF = HEAD_DIM // 2
KERNEL = 31
BLOCK = 128
BLOCKS = 32
LONG = 24
AWAY = -1e30
HERE = 256
SHARD = 384
EPSILON = 1e-05
MESH = pl.DeviceIdType.MESH
F32 = jnp.float32
BF16 = jnp.bfloat16


def rotation_tables():
    inverse = 10000.0 ** (-np.arange(HALF, dtype=np.float64) / HALF)
    angles = np.arange(LONG * BLOCK, dtype=np.float64)[None, :] * inverse[:, None]
    pair = np.stack([np.cos(angles), np.sin(angles)])
    pair = pair.reshape(2, HALF, LONG, BLOCK).transpose(2, 0, 1, 3)
    return np.ascontiguousarray(pair).astype(np.float32)


def norm(values, gain):
    average = jnp.mean(values, axis=-1, keepdims=True)
    centred = values - average
    variance = jnp.mean(centred * centred, axis=-1, keepdims=True)
    return centred * lax.rsqrt(variance + EPSILON) * gain


def flip(index, off):
    out = index
    for bit in (1, 2, 4):
        out = out + bit * ((off // bit) % 2) * (1 - 2 * ((index // bit) % 2))
    return out


def kernel(
    x_hbm, ids_hbm, attn_hbm, wqkv_hbm, wout_hbm, conv_hbm, cin_hbm, dw_hbm, depth_hbm, cout_hbm, tab_hbm,
    out_hbm,
    ids, attn_gain, conv_gain, depth_gain, dw, out, xv, wq, wo, cw, co, tab, normed, sq, skv, qbuf, kvbuf, kn, peaks, totals, osend, att, resid, filt, ext, tmp,
    load_sem, wq_sem, q_send, q_recv, kv_send, kv_recv, fwd_send, fwd_recv, o_send, o_recv,
    g_send, g_recv, s_send, s_recv, h_send, h_recv,
):
    d = lax.axis_index("dp")
    c = lax.axis_index("ctx")
    chip, core = c // 2, c % 2
    sibling = (d, c + 1 - 2 * core)
    z, yh = d // 2, d % 2
    zp, zm, z2 = (z + 1) % 4, (z + 3) % 4, (z + 2) % 4
    other = 1 - yh
    across = (2 * z + other, c + 2 - 4 * (chip % 2))
    up, down = (2 * zp + yh, c), (2 * zm + yh, c)
    right, left = (d, (c + 1) % 16), (d, (c + 15) % 16)

    def peer(off):
        return (d, 2 * flip(chip, off) + core)

    barrier = pltpu.get_barrier_semaphore()
    cross = (d, lax.select(core == 0, (c + 15) % 16, (c + 1) % 16))
    greeted = [peer(off) for off in range(1, 8)] + [sibling, across, up, down, cross]
    for device in greeted:
        pl.semaphore_signal(barrier, inc=1, device_id=device, device_id_type=MESH)

    def shard_cols(dd):
        return pl.ds(pl.multiple_of(SHARD * (2 * (dd % 4) + dd // 4), 128), SHARD)

    loads = [
        pltpu.make_async_copy(x_hbm.at[0], xv, load_sem.at[0]),
        pltpu.make_async_copy(tab_hbm, tab, load_sem.at[1]),
        pltpu.make_async_copy(wout_hbm, wo, load_sem.at[2]),
        pltpu.make_async_copy(cout_hbm, co, load_sem.at[3]),
        pltpu.make_async_copy(cin_hbm, cw.at[:, shard_cols(d)], load_sem.at[4]),
    ]
    small = [
        pltpu.make_async_copy(src, dst, load_sem.at[8 + n])
        for n, (src, dst) in enumerate(
            ((attn_hbm, attn_gain), (ids_hbm, ids), (conv_hbm, conv_gain), (depth_hbm, depth_gain), (dw_hbm, dw))
        )
    ]
    loads[0].start()
    small[0].start()
    small[1].start()
    far, near = 1 - chip // 4, chip // 4
    steps = ((0, far), (0, near), (1, far), (2, far), (1, near), (2, near))
    wq_copies = []
    for slot, (kind, group) in enumerate(steps):
        start = pl.multiple_of(768 * kind + SHARD * group, 128)
        copy = pltpu.make_async_copy(wqkv_hbm.at[:, pl.ds(start, SHARD)], wq.at[slot], wq_sem.at[slot])
        copy.start()
        wq_copies.append(copy)
        if slot == 0:
            loads[1].start()
    for copy in small[2:] + loads[2:]:
        copy.start()

    def remote(src, dst, device, ssem, rsem):
        return pltpu.make_async_remote_copy(
            src_ref=src, dst_ref=dst, send_sem=ssem, recv_sem=rsem, device_id=device, device_id_type=MESH
        )

    loads[0].wait()
    small[0].wait()

    def norm_rows(i, _):
        rows = pl.ds(pl.multiple_of(64 * i, 64), 64)
        normed[rows, :] = norm(xv[rows, :].astype(F32), attn_gain[...]).astype(BF16)
        return _

    lax.fori_loop(0, HERE // 64, norm_rows, 0)

    a_up, a_down, a_far = 2 * zp + yh, 2 * zm + yh, 2 * z2 + yh
    b_here, b_up, b_down, b_far = 2 * z + other, 2 * zp + other, 2 * zm + other, 2 * z2 + other

    def piece(dd, p, of=core):
        return cw.at[pl.ds(pl.multiple_of(768 * of + 384 * p, 384), 384), shard_cols(dd)]

    def third(dd, p, n):
        rows = pl.ds(pl.multiple_of(768 * core + 384 * p + 128 * n, 128), 128)
        return cw.at[rows, shard_cols(dd)]

    def gather(src, dst, device, p, n):
        return remote(src, dst, device, g_send.at[p, n], g_recv.at[p, n])

    def start_all(copies):
        for copy in copies:
            copy.start()

    def gather_wait(ref, p, n):
        remote(ref, ref, up, g_send.at[p, n], g_recv.at[p, n]).wait_recv()

    def to_sibling(dd, p, n):
        return remote(piece(dd, p), piece(dd, p), sibling, s_send.at[p, n], s_recv.at[p, n])

    def from_sibling(dd, n):
        for p in range(2):
            ref = piece(dd, p, 1 - core)
            remote(ref, ref, sibling, s_send.at[p, n], s_recv.at[p, n]).wait_recv()

    def gather_1(p):
        own = cin_hbm.at[pl.ds(pl.multiple_of(768 * core + 384 * p, 384), 384)]
        return [
            gather(own, piece(d, p), down, p, 0),
            gather(own, piece(d, p), across, p, 1),
            gather(own, piece(d, p), up, p, 2),
        ]

    def gather_2(p):
        return [
            gather(piece(a_up, p), piece(a_up, p), down, p, 3),
            gather(piece(a_up, p), piece(a_up, p), across, p, 4),
            gather(piece(b_here, p), piece(b_here, p), up, p, 5),
            to_sibling(a_up, p, 0),
            to_sibling(b_here, p, 1),
            to_sibling(a_down, p, 2),
        ]

    def gather_3(p):
        return [
            gather(third(a_far, p, 0), third(a_far, p, 0), across, p, 6),
            gather(third(b_up, p, 1), third(b_up, p, 1), down, p, 7),
            gather(third(b_down, p, 2), third(b_down, p, 2), up, p, 8),
            to_sibling(a_far, p, 3),
            to_sibling(b_up, p, 4),
            to_sibling(b_down, p, 5),
        ]

    def gather_4(p):
        return [to_sibling(b_far, p, 6)]

    def run_2(p):
        gather_wait(piece(a_up, p), p, 0)
        gather_wait(piece(b_here, p), p, 1)
        gather_wait(piece(a_down, p), p, 2)
        start_all(gather_2(p))

    def run_3(p):
        gather_wait(piece(a_far, p), p, 3)
        gather_wait(piece(b_up, p), p, 4)
        gather_wait(piece(b_down, p), p, 5)
        start_all(gather_3(p))

    def run_4(p):
        for n in range(3):
            gather_wait(third(b_far, p, n), p, 6 + n)
        start_all(gather_4(p))

    small[1].wait()
    place = []
    for t in range(2):
        mine = ids[0, 2 * c + t]
        earlier = jnp.int32(0)
        for j in range(BLOCKS):
            earlier = earlier + (ids[0, j] < mine).astype(jnp.int32)
        place.append(lax.min(2 * c + t - earlier, LONG - 1))
    loads[1].wait()
    cosine = jnp.concatenate([tab[place[0], 0], tab[place[1], 0]], axis=1)
    sine = jnp.concatenate([tab[place[0], 1], tab[place[1], 1]], axis=1)
    scale = math.log2(math.e) / math.sqrt(HEAD_DIM)

    def q_slot(i):
        return qbuf.at[i, pl.ds(0, HEAD_DIM)]

    def kv_slot(i, of):
        return kvbuf.at[i, :, pl.ds(0, HEAD_DIM), pl.ds(pl.multiple_of(HERE * of, HERE), HERE)]

    sends = []
    for slot, (kind, group) in enumerate(steps):
        wq_copies[slot].wait()
        turned = jnp.transpose(jnp.dot(normed[...], wq[slot], preferred_element_type=F32))
        for i in range(4):
            first = turned[96 * i : 96 * i + 48]
            second = turned[96 * i + 48 : 96 * i + 96]
            if kind < 2:
                first, second = first * cosine - second * sine, second * cosine + first * sine
            if kind == 0:
                sq[4 * group + i, 0:48, :] = (first * scale).astype(BF16)
                sq[4 * group + i, 48:96, :] = (second * scale).astype(BF16)
            else:
                skv[4 * group + i, kind - 1, 0:48, :] = first.astype(BF16)
                skv[4 * group + i, kind - 1, 48:96, :] = second.astype(BF16)
        if slot == 1:
            pl.semaphore_wait(barrier, len(greeted))
            for off in range(1, 8):
                to = flip(chip, off)
                sends.append(remote(sq.at[to], q_slot(chip), peer(off), q_send.at[off], q_recv.at[off]))
                sends[-1].start()
            start_all(gather_1(0))
            start_all(gather_1(1))
        if slot in (3, 5):
            for off in (range(4, 8) if slot == 3 else range(1, 4)):
                to = flip(chip, off)
                sends.append(remote(skv.at[to], kv_slot(chip, core), peer(off), kv_send.at[off], kv_recv.at[off]))
                sends[-1].start()
    keep_q = pltpu.make_async_copy(sq.at[chip], q_slot(chip), load_sem.at[5])
    keep_kv = pltpu.make_async_copy(skv.at[chip], kv_slot(chip, core), load_sem.at[6])
    keep_q.start()
    keep_kv.start()

    def forward(off, src):
        return remote(src, kv_slot(flip(chip, off), core), sibling, fwd_send.at[off], fwd_recv.at[off])

    forward(0, skv.at[chip]).start()

    row = lax.broadcasted_iota(jnp.int32, (BLOCK - HEAD_DIM, BLOCK), 0)

    def mark_keys(j, _):
        spot = pl.ds(pl.multiple_of(BLOCK * (j % 4), BLOCK), BLOCK)
        kvbuf[j // 4, 0, HEAD_DIM:, spot] = jnp.where(row == ids[0, j], 1.0, 0.0).astype(BF16)
        kvbuf[j // 4, 1, HEAD_DIM:, spot] = jnp.ones((BLOCK - HEAD_DIM, BLOCK), BF16)
        return _

    def mark_queries(j, _):
        spot = pl.ds(pl.multiple_of(BLOCK * (j % 2), BLOCK), BLOCK)
        mine = ids[0, 4 * (j // 2) + 2 * core + j % 2]
        qbuf[j // 2, HEAD_DIM:, spot] = jnp.where(row == mine, 0.0, AWAY).astype(BF16)
        return _

    lax.fori_loop(0, BLOCKS, mark_keys, 0)
    lax.fori_loop(0, 16, mark_queries, 0)
    peaks[...] = jnp.full(peaks.shape, -3e38, F32)
    totals[...] = jnp.zeros(totals.shape, F32)

    keep_q.wait()
    for off in range(1, 8):
        slot = q_slot(flip(chip, off))
        remote(slot, slot, peer(off), q_send.at[off], q_recv.at[off]).wait_recv()
    keep_kv.wait()

    def order(n):
        return lax.select(n < 5, n + 3, n - 4)

    def arrive(off):
        slot = kv_slot(flip(chip, off), core)
        remote(slot, slot, peer(off), kv_send.at[off], kv_recv.at[off]).wait_recv()
        forward(off, slot).start()

    def keys_of(off):
        source = flip(chip, off)
        slot = kv_slot(source, 1 - core)
        remote(slot, slot, sibling, fwd_send.at[off], fwd_recv.at[off]).wait_recv()
        kn[...] = jnp.transpose(kvbuf[source, 0])
        return source

    def attend(source, tiles, last=False):
        scores = [jnp.dot(kn[...], qbuf[i], preferred_element_type=F32) for i in tiles]
        results = []
        for i, score in zip(tiles, scores):
            old = peaks[i]
            top = jnp.maximum(old, jnp.max(score, axis=0, keepdims=True))
            if not last:
                peaks[i] = top
            weights = jnp.exp2(score - top).astype(BF16)
            fresh = jnp.dot(kvbuf[source, 1, 0:112, :], weights, preferred_element_type=F32)
            results.append(totals[i] * jnp.exp2(old - top) + fresh)
        return results

    def use_source(n, _):
        arrive(order(n + 1))
        pl.when(n == 2)(lambda: run_2(0))
        pl.when(n == 5)(lambda: run_2(1))
        source = keys_of(lax.select(n == 0, 0, order(n)))
        for i, total in enumerate(attend(source, range(8))):
            totals[i] = total
        return _

    lax.fori_loop(0, 7, use_source, 0)
    source = keys_of(order(7))

    def o_copy(i, off):
        return remote(osend.at[i], att.at[chip], (d, 2 * i + core), o_send.at[off], o_recv.at[off])

    for offs in ((6, 7, 4, 5), (2, 3, 1, 0)):
        tiles = [flip(chip, off) for off in offs]
        for off, i, total in zip(offs, tiles, attend(source, tiles, last=True)):
            osend[i] = (total[0:96] / total[96:97]).astype(BF16)
            if off:
                o_copy(i, off).start()
    o_keep = pltpu.make_async_copy(osend.at[chip], att.at[chip], load_sem.at[7])
    o_keep.start()

    run_3(0)
    loads[2].wait()
    o_keep.wait()
    for off in range(1, 8):
        slot = att.at[flip(chip, off)]
        remote(slot, slot, peer(off), o_send.at[off], o_recv.at[off]).wait_recv()
    normed[:, 0:768] = jnp.transpose(att[...].reshape(768, HERE))

    def add_out(i, _):
        cols = pl.ds(pl.multiple_of(512 * i, 512), 512)
        resid[:, cols] = xv[:, cols].astype(F32) + jnp.dot(
            normed[:, 0:768], wo[:, cols], preferred_element_type=F32
        )
        return _

    lax.fori_loop(0, 3, add_out, 0)
    run_3(1)

    small[2].wait()

    def norm_residual(i, _):
        rows = pl.ds(pl.multiple_of(64 * i, 64), 64)
        normed[rows, :] = norm(resid[rows, :], conv_gain[...]).astype(BF16)
        return _

    lax.fori_loop(0, HERE // 64, norm_residual, 0)

    def edge_copies(n, v):
        cols = pl.ds(pl.multiple_of(SHARD * v, 128), SHARD)
        return [
            remote(ext.at[pl.ds(256, 16), cols], ext.at[pl.ds(0, 16), cols], right, h_send.at[0, n], h_recv.at[0, n]),
            remote(ext.at[pl.ds(16, 16), cols], ext.at[pl.ds(272, 16), cols], left, h_send.at[1, n], h_recv.at[1, n]),
        ]

    edges = []

    def gate(n, v):
        cols = pl.ds(pl.multiple_of(SHARD * v, 128), SHARD)
        both = pl.ds(pl.multiple_of(2 * SHARD * v, 256), 2 * SHARD)
        wide = jnp.dot(normed[...], cw[:, both], preferred_element_type=F32)
        ext[16:272, cols] = (wide[:, :SHARD] * jax.nn.sigmoid(wide[:, SHARD:])).astype(BF16)
        for copy in edge_copies(n, v):
            copy.start()
            edges.append(copy)

    here_0, here_1 = ids[0, 2 * c], ids[0, 2 * c + 1]
    before = ids[0, lax.max(2 * c - 1, 0)]
    after = ids[0, lax.min(2 * c + 2, BLOCKS - 1)]
    inner = here_0 == here_1
    keeps = (
        (jnp.logical_and(c > 0, before == here_0), inner),
        (inner, jnp.logical_and(c < 15, after == here_1)),
    )

    def taps(n, v):
        for copy in edge_copies(n, v):
            copy.wait_recv()

        def filter_lanes(i, _):
            cols = pl.ds(pl.multiple_of(SHARD * v + BLOCK * i, BLOCK), BLOCK)
            for t in range(2):
                head = ext[BLOCK * t : BLOCK * t + 16, cols].astype(F32)
                tail = ext[BLOCK * t + 144 : BLOCK * t + 160, cols].astype(F32)
                tmp[t, 0:16, :] = jnp.where(keeps[t][0], head, 0.0)
                tmp[t, 16:144, :] = ext[BLOCK * t + 16 : BLOCK * t + 144, cols].astype(F32)
                tmp[t, 144:160, :] = jnp.where(keeps[t][1], tail, 0.0)
                total = jnp.zeros((BLOCK, BLOCK), F32)
                for tap in range(KERNEL):
                    total += dw[tap : tap + 1, cols] * tmp[t, tap + 1 : tap + 1 + BLOCK, :]
                filt[BLOCK * t : BLOCK * t + BLOCK, cols] = total
            return _

        lax.fori_loop(0, 3, filter_lanes, 0)

    groups = (a_up % 4, b_up % 4, d % 4, b_here % 4)
    for n in (0, 2):
        from_sibling((a_up, 0, a_down)[n], n)
    gate(0, groups[0])
    small[3].wait()
    small[4].wait()
    for n, dd in ((4, b_up), (5, b_down)):
        from_sibling(dd, n)
    gate(1, groups[1])
    run_4(0)
    loads[4].wait()
    from_sibling(a_far, 3)
    gate(2, groups[2])
    run_4(1)
    taps(0, groups[0])
    for n, dd in ((1, b_here), (6, b_far)):
        from_sibling(dd, n)
    gate(3, groups[3])
    for n in range(1, 4):
        taps(n, groups[n])

    def norm_filtered(i, _):
        rows = pl.ds(pl.multiple_of(64 * i, 64), 64)
        values = norm(filt[rows, :], depth_gain[...])
        normed[rows, :] = (values / (1.0 + jnp.exp(-values))).astype(BF16)
        return _

    lax.fori_loop(0, HERE // 64, norm_filtered, 0)

    loads[3].wait()

    def out_copy(i):
        cols = pl.ds(pl.multiple_of(512 * i, 512), 512)
        return pltpu.make_async_copy(out.at[:, cols], out_hbm.at[0, :, cols], load_sem.at[13 + i])

    def add_conv(i, _):
        cols = pl.ds(pl.multiple_of(512 * i, 512), 512)
        out[:, cols] = (
            resid[:, cols] + jnp.dot(normed[...], co[:, cols], preferred_element_type=F32)
        ).astype(BF16)
        out_copy(i).start()
        return _

    lax.fori_loop(0, 3, add_conv, 0)

    gathers = [copy for p in range(2) for step in (gather_1, gather_2, gather_3, gather_4) for copy in step(p)]
    for copy in gathers + sends + edges:
        copy.wait_send()
    forward(0, skv.at[chip]).wait_send()

    def drain(off, _):
        forward(off, kv_slot(flip(chip, off), core)).wait_send()
        o_copy(flip(chip, off), off).wait_send()
        return _

    lax.fori_loop(1, 8, drain, 0)
    for i in range(3):
        out_copy(i).wait()


def local(inputs, block_ids, attn_gain, w_qkv, w_out, conv_gain, conv_in, depthwise_w, depth_gain, conv_out):
    in_hbm = pl.BlockSpec(memory_space=pl.ANY)
    dma = pltpu.SemaphoreType.DMA
    return pl.pallas_call(
        kernel,
        out_shape=jax.ShapeDtypeStruct((1, HERE, MODEL_DIM), BF16),
        in_specs=[in_hbm] * 11,
        out_specs=in_hbm,
        scratch_shapes=[
            pltpu.SMEM((1, BLOCKS), jnp.int32),
            pltpu.VMEM((MODEL_DIM,), F32),
            pltpu.VMEM((MODEL_DIM,), F32),
            pltpu.VMEM((MODEL_DIM,), F32),
            pltpu.VMEM((KERNEL, MODEL_DIM), F32),
            pltpu.VMEM((HERE, MODEL_DIM), BF16),
            pltpu.VMEM((HERE, MODEL_DIM), BF16),
            pltpu.VMEM((6, MODEL_DIM, SHARD), BF16),
            pltpu.VMEM((768, MODEL_DIM), BF16),
            pltpu.VMEM((MODEL_DIM, 2 * MODEL_DIM), BF16),
            pltpu.VMEM((MODEL_DIM, MODEL_DIM), BF16),
            pltpu.VMEM((LONG, 2, HALF, BLOCK), F32),
            pltpu.VMEM((HERE, MODEL_DIM), BF16),
            pltpu.VMEM((8, HEAD_DIM, HERE), BF16),
            pltpu.VMEM((8, 2, HEAD_DIM, HERE), BF16),
            pltpu.VMEM((8, BLOCK, HERE), BF16),
            pltpu.VMEM((8, 2, BLOCK, 2 * HERE), BF16),
            pltpu.VMEM((2 * HERE, BLOCK), BF16),
            pltpu.VMEM((8, 1, HERE), F32),
            pltpu.VMEM((8, 112, HERE), F32),
            pltpu.VMEM((8, HEAD_DIM, HERE), BF16),
            pltpu.VMEM((8, HEAD_DIM, HERE), BF16),
            pltpu.VMEM((HERE, MODEL_DIM), F32),
            pltpu.VMEM((HERE, MODEL_DIM), F32),
            pltpu.VMEM((HERE + 32, MODEL_DIM), BF16),
            pltpu.VMEM((2, 160, BLOCK), F32),
            dma((16,)), dma((6,)), dma((8,)), dma((8,)), dma((8,)), dma((8,)), dma((8,)), dma((8,)), dma((8,)), dma((8,)),
            dma((2, 9)), dma((2, 9)), dma((2, 7)), dma((2, 7)), dma((2, 4)), dma((2, 4)),
        ],
        compiler_params=pltpu.CompilerParams(
            collective_id=0, has_side_effects=True, vmem_limit_bytes=56 * 1024 * 1024
        ),
        name="conformer",
    )(
        inputs, block_ids, attn_gain, w_qkv, w_out, conv_gain, conv_in, depthwise_w,
        depth_gain, conv_out, jnp.asarray(rotation_tables()),
    )


def solution(mesh):
    return jax.shard_map(
        local,
        mesh=mesh,
        in_specs=(
            P("dp", "ctx", None),
            P("dp", None),
            P(),
            P(),
            P(),
            P(),
            P(None, "dp"),
            P(),
            P(),
            P(),
        ),
        out_specs=P("dp", "ctx", None),
        check_vma=False,
    )
```

profile of v0, /device:TPU:0, one launch (start us, length us, event | category | flops | bytes accessed | tf_op | source)
XLA Modules:
  0.0 57.4 jit_solution(17391110619974380358)
XLA Ops:
  0.0 55.4 %conformer.1 = bf16[1,256,1536]{2,1,0:T(8,128)(2,1)} custom-call(bf16[1,256,1536]{2,1,0:T(8,128)(2,1)} %x_hbm.1, s32[1,32]{1,0:T(1,128)} %ids_hbm.1, f32[1536]{0:T(1024)} %attn_hbm.1, bf16[1536,2304]{1,0:T(8,128)(2,1)} %wqkv_hbm.1, bf16[768,1536]{1,0:T(8,128)(2,1)} %wout_hbm.1, f32[1536]{0:T(1024)} %conv_hbm.1, bf16[1536,384]{1,0:T(8,128)(2,1)} %cin_hbm.1, ...), custom_call_target="tpu_custom_call" | custom-call | tf_op jit(solution)/shard_map/conformer/pallas_call | solution.py:472
  55.4 2.1 %copy.13 = bf16[1,256,1536]{2,1,0:T(8,128)(2,1)} copy(bf16[1,256,1536]{2,1,0:T(8,128)(2,1)} %conformer.1) | data formatting | bytes 1572864
where the time goes:
time: 57.6 us; the launch traced here: 57.4 us
  Pallas kernels  55.4 us (96%)
  local copies, waits for them, and re-layouts  2.06 us (4%)
    pallas_call x1, Pallas kernels, local(): pl.pallas_call(kernel, out_shape=jax.ShapeDtypeStruct((1, HERE, MODEL_DIM...  55.4 us
    unnamed x1, local copies, waits for them, and re-layouts  2.06 us

commit v1 on v0

--- a/solution.py
+++ b/solution.py
@@ -116,11 +116,11 @@
     small[0].wait()
 
     def norm_rows(i, _):
-        rows = pl.ds(pl.multiple_of(64 * i, 64), 64)
+        rows = pl.ds(pl.multiple_of(128 * i, 128), 128)
         normed[rows, :] = norm(xv[rows, :].astype(F32), attn_gain[...]).astype(BF16)
         return _
 
-    lax.fori_loop(0, HERE // 64, norm_rows, 0)
+    lax.fori_loop(0, HERE // 128, norm_rows, 0)
 
     a_up, a_down, a_far = 2 * zp + yh, 2 * zm + yh, 2 * z2 + yh
     b_here, b_up, b_down, b_far = 2 * z + other, 2 * zp + other, 2 * zm + other, 2 * z2 + other
@@ -353,11 +353,11 @@
     small[2].wait()
 
     def norm_residual(i, _):
-        rows = pl.ds(pl.multiple_of(64 * i, 64), 64)
+        rows = pl.ds(pl.multiple_of(128 * i, 128), 128)
         normed[rows, :] = norm(resid[rows, :], conv_gain[...]).astype(BF16)
         return _
 
-    lax.fori_loop(0, HERE // 64, norm_residual, 0)
+    lax.fori_loop(0, HERE // 128, norm_residual, 0)
 
     def edge_copies(n, v):
         cols = pl.ds(pl.multiple_of(SHARD * v, 128), SHARD)
@@ -428,12 +428,12 @@
         taps(n, groups[n])
 
     def norm_filtered(i, _):
-        rows = pl.ds(pl.multiple_of(64 * i, 64), 64)
+        rows = pl.ds(pl.multiple_of(128 * i, 128), 128)
         values = norm(filt[rows, :], depth_gain[...])
         normed[rows, :] = (values / (1.0 + jnp.exp(-values))).astype(BF16)
         return _
 
-    lax.fori_loop(0, HERE // 64, norm_filtered, 0)
+    lax.fori_loop(0, HERE // 128, norm_filtered, 0)
 
     loads[3].wait()
 

time: 57.6 us -> 56.9 us (0.988)
  Pallas kernels: 55.4 us -> 54.7 us
    pallas_call x1, Pallas kernels: 55.4 us -> 54.7 us  [local(): pl.pallas_call(kernel, out_shape=jax.ShapeDtypeStruct((1, HERE, MODEL_DIM...]
where the time goes in v1:
time: 56.9 us; the launch traced here: 56.8 us
  Pallas kernels  54.7 us (96%)
  local copies, waits for them, and re-layouts  2.06 us (4%)
    pallas_call x1, Pallas kernels, local(): pl.pallas_call(kernel, out_shape=jax.ShapeDtypeStruct((1, HERE, MODEL_DIM...  54.7 us
    unnamed x1, local copies, waits for them, and re-layouts  2.06 us

profile of v1, /device:TPU:0, one launch (start us, length us, event | category | flops | bytes accessed | tf_op | source)
XLA Modules:
  0.0 56.8 jit_solution(16539957563935837287)
XLA Ops:
  0.0 54.7 %conformer.1 = bf16[1,256,1536]{2,1,0:T(8,128)(2,1)} custom-call(bf16[1,256,1536]{2,1,0:T(8,128)(2,1)} %x_hbm.1, s32[1,32]{1,0:T(1,128)} %ids_hbm.1, f32[1536]{0:T(1024)} %attn_hbm.1, bf16[1536,2304]{1,0:T(8,128)(2,1)} %wqkv_hbm.1, bf16[768,1536]{1,0:T(8,128)(2,1)} %wout_hbm.1, f32[1536]{0:T(1024)} %conv_hbm.1, bf16[1536,384]{1,0:T(8,128)(2,1)} %cin_hbm.1, ...), custom_call_target="tpu_custom_call" | custom-call | tf_op jit(solution)/shard_map/conformer/pallas_call | solution.py:472
  54.7 2.1 %copy.13 = bf16[1,256,1536]{2,1,0:T(8,128)(2,1)} copy(bf16[1,256,1536]{2,1,0:T(8,128)(2,1)} %conformer.1) | data formatting | bytes 1572864

commit v2 on v1

--- a/solution.py
+++ b/solution.py
@@ -116,11 +116,11 @@
     small[0].wait()
 
     def norm_rows(i, _):
-        rows = pl.ds(pl.multiple_of(128 * i, 128), 128)
+        rows = pl.ds(pl.multiple_of(256 * i, 256), 256)
         normed[rows, :] = norm(xv[rows, :].astype(F32), attn_gain[...]).astype(BF16)
         return _
 
-    lax.fori_loop(0, HERE // 128, norm_rows, 0)
+    lax.fori_loop(0, HERE // 256, norm_rows, 0)
 
     a_up, a_down, a_far = 2 * zp + yh, 2 * zm + yh, 2 * z2 + yh
     b_here, b_up, b_down, b_far = 2 * z + other, 2 * zp + other, 2 * zm + other, 2 * z2 + other
@@ -353,11 +353,11 @@
     small[2].wait()
 
     def norm_residual(i, _):
-        rows = pl.ds(pl.multiple_of(128 * i, 128), 128)
+        rows = pl.ds(pl.multiple_of(256 * i, 256), 256)
         normed[rows, :] = norm(resid[rows, :], conv_gain[...]).astype(BF16)
         return _
 
-    lax.fori_loop(0, HERE // 128, norm_residual, 0)
+    lax.fori_loop(0, HERE // 256, norm_residual, 0)
 
     def edge_copies(n, v):
         cols = pl.ds(pl.multiple_of(SHARD * v, 128), SHARD)
@@ -428,12 +428,12 @@
         taps(n, groups[n])
 
     def norm_filtered(i, _):
-        rows = pl.ds(pl.multiple_of(128 * i, 128), 128)
+        rows = pl.ds(pl.multiple_of(256 * i, 256), 256)
         values = norm(filt[rows, :], depth_gain[...])
         normed[rows, :] = (values / (1.0 + jnp.exp(-values))).astype(BF16)
         return _
 
-    lax.fori_loop(0, HERE // 128, norm_filtered, 0)
+    lax.fori_loop(0, HERE // 256, norm_filtered, 0)
 
     loads[3].wait()
 

time: 56.9 us -> 56.8 us (level)
  no operation moved by 1% of the time
where the time goes in v2:
time: 56.8 us; the launch traced here: 56.7 us
  Pallas kernels  54.6 us (96%)
  local copies, waits for them, and re-layouts  2.06 us (4%)
    pallas_call x1, Pallas kernels, local(): pl.pallas_call(kernel, out_shape=jax.ShapeDtypeStruct((1, HERE, MODEL_DIM...  54.6 us
    unnamed x1, local copies, waits for them, and re-layouts  2.06 us

profile of v2, /device:TPU:0, one launch (start us, length us, event | category | flops | bytes accessed | tf_op | source)
XLA Modules:
  0.0 56.7 jit_solution(17214244189642613780)
XLA Ops:
  0.0 54.6 %conformer.1 = bf16[1,256,1536]{2,1,0:T(8,128)(2,1)} custom-call(bf16[1,256,1536]{2,1,0:T(8,128)(2,1)} %x_hbm.1, s32[1,32]{1,0:T(1,128)} %ids_hbm.1, f32[1536]{0:T(1024)} %attn_hbm.1, bf16[1536,2304]{1,0:T(8,128)(2,1)} %wqkv_hbm.1, bf16[768,1536]{1,0:T(8,128)(2,1)} %wout_hbm.1, f32[1536]{0:T(1024)} %conv_hbm.1, bf16[1536,384]{1,0:T(8,128)(2,1)} %cin_hbm.1, ...), custom_call_target="tpu_custom_call" | custom-call | tf_op jit(solution)/shard_map/conformer/pallas_call | solution.py:472
  54.6 2.1 %copy.13 = bf16[1,256,1536]{2,1,0:T(8,128)(2,1)} copy(bf16[1,256,1536]{2,1,0:T(8,128)(2,1)} %conformer.1) | data formatting | bytes 1572864

commit v3 on v2

--- a/solution.py
+++ b/solution.py
@@ -340,14 +340,14 @@
         remote(slot, slot, peer(off), o_send.at[off], o_recv.at[off]).wait_recv()
     normed[:, 0:768] = jnp.transpose(att[...].reshape(768, HERE))
 
-    def add_out(i, _):
-        cols = pl.ds(pl.multiple_of(512 * i, 512), 512)
+    def add_out(i):
+        cols = slice(512 * i, 512 * i + 512)
         resid[:, cols] = xv[:, cols].astype(F32) + jnp.dot(
             normed[:, 0:768], wo[:, cols], preferred_element_type=F32
         )
-        return _
-
-    lax.fori_loop(0, 3, add_out, 0)
+
+    for i in range(3):
+        add_out(i)
     run_3(1)
 
     small[2].wait()
@@ -438,18 +438,18 @@
     loads[3].wait()
 
     def out_copy(i):
-        cols = pl.ds(pl.multiple_of(512 * i, 512), 512)
+        cols = pl.ds(512 * i, 512)
         return pltpu.make_async_copy(out.at[:, cols], out_hbm.at[0, :, cols], load_sem.at[13 + i])
 
-    def add_conv(i, _):
-        cols = pl.ds(pl.multiple_of(512 * i, 512), 512)
+    def add_conv(i):
+        cols = slice(512 * i, 512 * i + 512)
         out[:, cols] = (
             resid[:, cols] + jnp.dot(normed[...], co[:, cols], preferred_element_type=F32)
         ).astype(BF16)
         out_copy(i).start()
-        return _
-
-    lax.fori_loop(0, 3, add_conv, 0)
+
+    for i in range(3):
+        add_conv(i)
 
     gathers = [copy for p in range(2) for step in (gather_1, gather_2, gather_3, gather_4) for copy in step(p)]
     for copy in gathers + sends + edges:

time: 56.8 us -> 56 us (0.986)
  Pallas kernels: 54.6 us -> 53.8 us
    pallas_call x1, Pallas kernels: 54.6 us -> 53.8 us  [local(): pl.pallas_call(kernel, out_shape=jax.ShapeDtypeStruct((1, HERE, MODEL_DIM...]
where the time goes in v3:
time: 56 us; the launch traced here: 55.9 us
  Pallas kernels  53.8 us (96%)
  local copies, waits for them, and re-layouts  2.06 us (4%)
    pallas_call x1, Pallas kernels, local(): pl.pallas_call(kernel, out_shape=jax.ShapeDtypeStruct((1, HERE, MODEL_DIM...  53.8 us
    unnamed x1, local copies, waits for them, and re-layouts  2.06 us

profile of v3, /device:TPU:0, one launch (start us, length us, event | category | flops | bytes accessed | tf_op | source)
XLA Modules:
  0.0 55.9 jit_solution(9591050345166620045)
XLA Ops:
  0.0 53.8 %conformer.1 = bf16[1,256,1536]{2,1,0:T(8,128)(2,1)} custom-call(bf16[1,256,1536]{2,1,0:T(8,128)(2,1)} %x_hbm.1, s32[1,32]{1,0:T(1,128)} %ids_hbm.1, f32[1536]{0:T(1024)} %attn_hbm.1, bf16[1536,2304]{1,0:T(8,128)(2,1)} %wqkv_hbm.1, bf16[768,1536]{1,0:T(8,128)(2,1)} %wout_hbm.1, f32[1536]{0:T(1024)} %conv_hbm.1, bf16[1536,384]{1,0:T(8,128)(2,1)} %cin_hbm.1, ...), custom_call_target="tpu_custom_call" | custom-call | tf_op jit(solution)/shard_map/conformer/pallas_call | solution.py:472
  53.8 2.1 %copy.13 = bf16[1,256,1536]{2,1,0:T(8,128)(2,1)} copy(bf16[1,256,1536]{2,1,0:T(8,128)(2,1)} %conformer.1) | data formatting | bytes 1572864

commit v4 on v3

--- a/solution.py
+++ b/solution.py
@@ -404,7 +404,8 @@
                 filt[BLOCK * t : BLOCK * t + BLOCK, cols] = total
             return _
 
-        lax.fori_loop(0, 3, filter_lanes, 0)
+        for i in range(3):
+            filter_lanes(i, 0)
 
     groups = (a_up % 4, b_up % 4, d % 4, b_here % 4)
     for n in (0, 2):

time: 56 us -> 56.1 us (level)
  no operation moved by 1% of the time
where the time goes in v4:
time: 56.1 us; the launch traced here: 55.9 us
  Pallas kernels  53.9 us (96%)
  local copies, waits for them, and re-layouts  2.06 us (4%)
    pallas_call x1, Pallas kernels, local(): pl.pallas_call(kernel, out_shape=jax.ShapeDtypeStruct((1, HERE, MODEL_DIM...  53.9 us
    unnamed x1, local copies, waits for them, and re-layouts  2.06 us

profile of v4, /device:TPU:0, one launch (start us, length us, event | category | flops | bytes accessed | tf_op | source)
XLA Modules:
  0.0 55.9 jit_solution(10409762197122336524)
XLA Ops:
  0.0 53.9 %conformer.1 = bf16[1,256,1536]{2,1,0:T(8,128)(2,1)} custom-call(bf16[1,256,1536]{2,1,0:T(8,128)(2,1)} %x_hbm.1, s32[1,32]{1,0:T(1,128)} %ids_hbm.1, f32[1536]{0:T(1024)} %attn_hbm.1, bf16[1536,2304]{1,0:T(8,128)(2,1)} %wqkv_hbm.1, bf16[768,1536]{1,0:T(8,128)(2,1)} %wout_hbm.1, f32[1536]{0:T(1024)} %conv_hbm.1, bf16[1536,384]{1,0:T(8,128)(2,1)} %cin_hbm.1, ...), custom_call_target="tpu_custom_call" | custom-call | tf_op jit(solution)/shard_map/conformer/pallas_call | solution.py:473
  53.9 2.1 %copy.13 = bf16[1,256,1536]{2,1,0:T(8,128)(2,1)} copy(bf16[1,256,1536]{2,1,0:T(8,128)(2,1)} %conformer.1) | data formatting | bytes 1572864
